TPU v7x, 512 devices: a whole 4x8x8 slice. The times are simulated.
512 devices in a mesh: expert: 64 (over z, y), tensor: 4 (over x), dp: 2 (over core).
Axes of the slice: x: 4, y: 8, z: 8, core: 2. Of those that a mesh axis runs over, the one named last changes fastest.
Arguments:
- tokens: bfloat16 [4096, 3584], P(('dp', 'expert'), 'tensor'), parts along dimension 0, may hold values from -6 to 6
- dither: int32 [4096], P(('dp', 'expert')), parts along dimension 0, may hold values from 0 to 255
- expert_ids: int32 [4096, 8], P(('dp', 'expert')), parts along dimension 0, may hold values from 0 to 31, all different within a row; in each aligned block of 32 rows (0 to 31, 32 to 63, ...) at most 16 rows name the same one
- gate_values: float32 [4096, 8], P(('dp', 'expert')), parts along dimension 0, may hold values from 0.05 to 0.5
- gate_weight: bfloat16 [64, 3584, 512], P('expert', None, 'tensor'), may hold values from -0.09375 to 0.09375
- up_weight: bfloat16 [64, 3584, 512], P('expert', None, 'tensor'), may hold values from -0.09375 to 0.09375
- down_weight: bfloat16 [64, 512, 3584], P('expert', None, 'tensor'), may hold values from -0.1875 to 0.1875
Outputs:
- moe_output: bfloat16 [4096, 3584], P(('dp', 'expert'), 'tensor'), parts along dimension 0
There are 2 independent parts, one for each index of `dp`. A program takes and returns all parts, laid end to end along the dimension named above; an argument that names none is the same for every part. Nothing has to cross between parts.
Inputs may be any that keep to these rules, and one draw needn't show every extreme that they name: `expert_ids`: each row names 8 different experts. Among the 32 rows of one index of the expert axis no expert is named more than 16 times, a bound that some block reaches.
All inputs are finite; a program needn't handle non-finite values.
Results may differ from a plain program's by a relative error of at most 0.0057.
Values may be sent and summed in bfloat16 or wider, within the bound.
A program may use at most 64 MiB of HBM per device.

v0:
```python
import jax
import jax.numpy as jnp
from jax import lax
from jax.sharding import PartitionSpec as P


def dither_round(values, dither, column_start):
    scaled = values.astype(jnp.float32)
    magnitude = jnp.abs(scaled)
    grid_step = jnp.full_like(scaled, 2.0 ** (-26))
    for octave in range(-23, 4):
        grid_step = grid_step + jnp.where(magnitude >= 2.0**octave, 2.0 ** (octave - 3), 0.0)
    columns = column_start + jnp.arange(scaled.shape[1], dtype=jnp.int32)
    offset = (dither[:, None] + 97 * columns[None, :]) % 256
    jitter = (offset.astype(jnp.float32) + 0.5) / 256.0
    return (jnp.floor(scaled / grid_step + jitter) * grid_step).astype(jnp.bfloat16)


def on_device(tokens, dither, expert_ids, gate_values, gate_weight, up_weight, down_weight):
    quarter = tokens.shape[1]
    full_width = quarter * lax.axis_size("tensor")
    tok_rows = tokens.shape[0]
    topk_count = expert_ids.shape[1]
    experts_total = lax.axis_size("expert") // 2
    capacity = min(tok_rows, 2 * tok_rows * topk_count // experts_total)
    rounded = dither_round(tokens, dither, lax.axis_index("tensor") * quarter)
    flat_ids = expert_ids.reshape(-1)
    onehot = (flat_ids[:, None] == jnp.arange(experts_total, dtype=jnp.int32)[None, :]).astype(
        jnp.int32
    )
    before = jnp.cumsum(onehot, axis=0) - onehot
    slot_index = jnp.sum(before * onehot, axis=1)
    target = (flat_ids * capacity + slot_index).reshape(tok_rows, topk_count)
    slot_ids = jnp.arange(experts_total * capacity, dtype=jnp.int32)
    placement = jnp.any(slot_ids[:, None, None] == target[None, :, :], axis=2).astype(jnp.bfloat16)
    gate_own = gate_weight[0]
    up_own = up_weight[0]
    down_own = down_weight[0]
    whole_rows = lax.all_gather(rounded, "tensor", axis=1, tiled=True)
    packed = jnp.dot(placement, whole_rows, preferred_element_type=jnp.float32).astype(jnp.bfloat16)
    packed = packed.reshape(experts_total, 1, capacity, full_width)
    outgoing = jnp.broadcast_to(packed, (experts_total, 2, capacity, full_width))
    outgoing = outgoing.reshape(2 * experts_total, capacity, full_width)
    arrived_rows = lax.all_to_all(outgoing, "expert", split_axis=0, concat_axis=0, tiled=True)
    slot_count = arrived_rows.shape[1]
    rows_in = arrived_rows.reshape(-1, full_width)
    gate_pre = jnp.dot(rows_in, gate_own, preferred_element_type=jnp.float32)
    up_pre = jnp.dot(rows_in, up_own, preferred_element_type=jnp.float32)
    hidden = (jax.nn.silu(gate_pre) * up_pre).astype(jnp.bfloat16)
    hidden_all = lax.all_gather(hidden, "tensor", axis=1, tiled=True)
    result = jnp.dot(hidden_all, down_own, preferred_element_type=jnp.float32).astype(jnp.bfloat16)
    result = result.reshape(-1, slot_count, quarter)
    returned = lax.all_to_all(result, "expert", split_axis=0, concat_axis=0, tiled=True)
    pair_total = returned.astype(jnp.float32).reshape(experts_total, 2, capacity, quarter)
    pair_total = jnp.sum(pair_total, axis=1).reshape(experts_total * capacity, quarter)
    picked = pair_total[target]
    combined = jnp.sum(gate_values[:, :, None] * picked, axis=1)
    return combined.astype(jnp.bfloat16)


def solution(mesh):
    in_specs = (
        P(("dp", "expert"), "tensor"),
        P(("dp", "expert")),
        P(("dp", "expert"), None),
        P(("dp", "expert"), None),
        P("expert", None, "tensor"),
        P("expert", None, "tensor"),
        P("expert", None, "tensor"),
    )
    out_specs = P(("dp", "expert"), "tensor")
    return jax.shard_map(
        on_device, mesh=mesh, in_specs=in_specs, out_specs=out_specs, check_vma=False
    )
```

profile of v0, /device:TPU:4, one launch (start us, length us, event | category | flops | bytes accessed | tf_op | source)
XLA Modules:
  0.0 317.6 jit_solution(14163012201152307625)
XLA Ops:
  6.5 0.0 copy-start
  6.5 0.0 all-gather.2.cloned.1.call-start
  6.5 0.8 copy.16
  7.4 0.1 eq.45
  7.5 0.1 eq.41
  7.6 0.6 reduce-window.6
  8.2 0.2 slice_reduce_fusion
  8.4 0.1 fusion.44
  8.5 0.1 reduce_sum.30
  8.6 0.2 fusion.6
  8.9 1.2 fusion.41
  10.1 16.0 %all_gather.6 = bf16[32,3584]{1,0:T(8,128)(2,1)S(1)} all-gather(bf16[32,896]{1,0:T(8,128)(2,1)S(1)} %fusion.41), channel_id=1, replica_groups=mesh['expert'=64,'tensor'=4,'dp'=2] {'tensor'}, dimensions={1}, use_global_device_ids=true | all-gather | bytes 286720 | tf_op jit(solution)/shard_map/all_gather | solution.py:39
  26.1 1.2 convolution_convert_fusion
  27.3 0.9 broadcast_in_dim.85
  28.2 0.0 copy-start.2
  28.2 173.9 %all_to_all.10 = bf16[64,16,3584]{2,1,0:T(8,128)(2,1)S(1)} all-to-all(bf16[64,16,3584]{2,1,0:T(8,128)(2,1)S(1)} %bitcast.46), channel_id=1, replica_groups=mesh['expert'=64,'tensor'=4,'dp'=2] {'expert'}, dimensions={0} | all-to-all | bytes 14680064 | tf_op jit(solution)/shard_map/all_to_all | solution.py:44
  202.1 0.0 copy-done.2
  202.1 2.1 fusion.4
  204.1 0.0 copy-done.3
  204.2 2.8 fusion
  206.9 0.0 all-gather.2.cloned.1.call-update
  206.9 34.1 %all-gather.2.cloned.1.call-done = bf16[1024,512]{1,0:T(8,128)(2,1)} async-done(((bf16[1024,128]{1,0:T(8,128)(2,1)}), bf16[1024,512]{1,0:T(8,128)(2,1)}) %all-gather.2.cloned.1.call-update) | async-done | bytes 1048592 | tf_op jit(solution)/shard_map/all_gather | solution.py:50
  241.1 0.0 copy-done
  241.1 3.7 %convolution_convert_fusion.1 = bf16[1024,896]{1,0:T(8,128)(2,1)} fusion(bf16[1024,512]{1,0:T(8,128)(2,1)} %all-gather.2.cloned.1.call-done, bf16[1,512,896]{2,1,0:T(8,128)(2,1)S(1)} %copy-done), kind=kOutput, calls=%fused_computation.3 | convolution fusion | flops 940441600 | bytes 3801088 | tf_op jit(solution)/shard_map/dot_general | solution.py:51
  244.8 13.6 %all-to-all-start.1 = ((bf16[64,16,896]{2,1,0:T(8,128)(2,1)}), bf16[64,16,896]{2,1,0:T(8,128)(2,1)}, u32[]{:S(2)}, u32[]{:S(2)}) async-start(bf16[64,16,896]{2,1,0:T(8,128)(2,1)} %bitcast.7), calls=%async_computation.1 | async-start | bytes 3670016 | tf_op jit(solution)/shard_map/all_to_all | solution.py:53
  258.5 0.1 reshape.65
  258.5 0.0 copy-done.1
  258.6 0.1 copy.15
  258.6 46.0 %all-to-all-done.1 = bf16[64,16,896]{2,1,0:T(8,128)(2,1)} async-done(((bf16[64,16,896]{2,1,0:T(8,128)(2,1)}), bf16[64,16,896]{2,1,0:T(8,128)(2,1)}, u32[]{:S(2)}, u32[]{:S(2)}) %all-to-all-start.1) | async-done | bytes 1835040 | tf_op jit(solution)/shard_map/all_to_all | solution.py:53
  304.7 2.0 convert_reduce_fusion
  306.7 2.0 gather_fusion
  308.7 2.1 fusion.1
  (8 shorter events, 0.1 us)
Async XLA Ops:
  6.5 234.5 %copy-start = (bf16[1,512,896]{2,1,0:T(8,128)(2,1)S(1)}, bf16[1,512,896]{2,1,0:T(8,128)(2,1)}, u32[]{:S(2)}) copy-start(bf16[1,512,896]{2,1,0:T(8,128)(2,1)} %param.13) | copy-start | bytes 2752516
  6.5 234.5 %all-gather.2.cloned.1.call-start = ((), (), s32[]{:S(2)}) async-start(), calls=%async_computation.2 | async-start | bytes 1310720 | tf_op jit(solution)/shard_map/all_gather | solution.py:50
  28.2 173.9 %copy-start.2 = (bf16[1,3584,128]{2,1,0:T(8,128)(2,1)S(1)}, bf16[1,3584,128]{2,1,0:T(8,128)(2,1)}, u32[]{:S(2)}) copy-start(bf16[1,3584,128]{2,1,0:T(8,128)(2,1)} %param.11) | copy-start | bytes 2752516
  202.1 2.1 copy-start.3
  244.8 13.7 %copy-start.1 = (f32[32,8]{0,1:T(8,128)S(1)}, f32[32,8]{0,1:T(8,128)}, u32[]{:S(2)}) copy-start(f32[32,8]{0,1:T(8,128)} %param.10) | copy-start | bytes 3076
  244.8 59.9 %all-to-all-start.1 = ((bf16[64,16,896]{2,1,0:T(8,128)(2,1)}), bf16[64,16,896]{2,1,0:T(8,128)(2,1)}, u32[]{:S(2)}, u32[]{:S(2)}) async-start(bf16[64,16,896]{2,1,0:T(8,128)(2,1)} %bitcast.7), calls=%async_computation.1 | async-start | bytes 3670016 | tf_op jit(solution)/shard_map/all_to_all | solution.py:53
Sparse Core Ops, SparseCore 0:
  207.1 33.9 all-gather.1
where the time goes:
time: 318 us
  blocking collectives  190 us (60%)
  waiting for transfers between devices  80.2 us (25%)
  starting transfers between devices  13.7 us (4%)
  between operations  13.5 us (4%)
  matrix products  9.69 us (3%)
  other arithmetic  6.35 us (2%)
  local copies, waits for them, and re-layouts  4.36 us (1%)
    all_to_all x1, blocking collectives, on_device(): lax.all_to_all(outgoing, 'expert', split_axis=0, concat_axis=0, tiled=True)  174 us
    all_to_all x1, waiting for transfers between devices, on_device(): lax.all_to_all(result, 'expert', split_axis=0, concat_axis=0, tiled=True)  46 us
    all_gather x1, waiting for transfers between devices, on_device(): hidden_all = lax.all_gather(hidden, 'tensor', axis=1, tiled=True)  34.1 us
    all_gather x1, blocking collectives, on_device(): whole_rows = lax.all_gather(rounded, 'tensor', axis=1, tiled=True)  16 us
    all_to_all x1, starting transfers between devices, on_device(): lax.all_to_all(result, 'expert', split_axis=0, concat_axis=0, tiled=True)  13.6 us
  transfers between devices with their start and end apart: 2, of which 2 were waited for; matrix products, arithmetic and copies ran while one was open for 0% of the time, Pallas kernels for 0%

commit v1 on v0

v1 whole, which is shorter than its diff:
```python
import functools

import jax
import jax.numpy as jnp
from jax import lax
from jax.experimental import pallas as pl
from jax.experimental.pallas import tpu as pltpu
from jax.sharding import PartitionSpec as P

MESH = pl.DeviceIdType.MESH
BF = jnp.bfloat16
F32 = jnp.float32
N = 8
X = 4
HALF = 16
GROUPS = 8
CUT = 512


def iota(shape, axis):
    return lax.broadcasted_iota(jnp.int32, shape, axis)


def dither_round(values, dither_row, column_start):
    rows, cols = values.shape
    scaled = values.astype(F32)
    magnitude = jnp.abs(scaled)
    grid = jnp.full_like(scaled, 2.0**-26)
    inverse = jnp.full_like(scaled, 2.0**26)
    for octave in range(-23, 4):
        above = magnitude >= 2.0**octave
        grid = jnp.where(above, 2.0 ** (octave - 2), grid)
        inverse = jnp.where(above, 2.0 ** (2 - octave), inverse)
    square = jnp.broadcast_to(dither_row.astype(F32), (rows, rows))
    diagonal = iota((rows, rows), 0) == iota((rows, rows), 1)
    column = jnp.sum(jnp.where(diagonal, square, 0.0), axis=1, keepdims=True).astype(jnp.int32)
    offset = (column + 97 * (column_start + iota((rows, cols), 1))) & 255
    jitter = (offset.astype(F32) + 0.5) / 256.0
    return (jnp.floor(scaled * inverse + jitter) * grid).astype(BF)


def gate_table(ids, gates):
    rows = []
    lane = iota((HALF, 128), 1)
    own = lane % HALF == iota((HALF, 128), 0)
    for r in range(8):
        part = slice((r // 4) * HALF, (r // 4) * HALF + HALF)
        expert = (r % 4) * 8 + lane // HALF
        total = jnp.zeros((HALF, 128), F32)
        for k in range(ids.shape[1]):
            total = total + jnp.where(ids[part, k : k + 1] == expert, gates[part, k : k + 1], 0.0)
        rows.append(jnp.sum(jnp.where(own, total, 0.0), axis=0, keepdims=True))
    return jnp.concatenate(rows, axis=0)


def group_of(n):
    return jnp.where(n % 2 == 1, 4 - (n + 1) // 2, 4 + n // 2)


def kernel(
    tok, dit, ids, gat, gw, uw, dw, out,
    XA, XB, AUX, WX, WF, WD, PT, GS, OWN, NB, SX, T1, R2, HB, CA, RA, CB, RB, FA, FB, SA, SB, TA, TB,
    ag_s, ag_r, w_s, w_r, w_l, x_s, x_r, ra_s, ra_r, b_s, b_r, fa_s, fa_r, fb_s, fb_r,
):
    here = lax.axis_index("expert")
    t = lax.axis_index("tensor")
    c = lax.axis_index("dp")
    y, z = here % N, here // N
    e = here // 2

    def ydev(k):
        return {"expert": z * N + (y + k + N) % N}

    def zdev(k):
        return {"expert": ((z + k + N) % N) * N + y}

    def xdev(k):
        return {"tensor": (t + k + X) % X}

    def copy(src, dst, ss, rs, dev):
        return pltpu.make_async_remote_copy(
            src_ref=src, dst_ref=dst, send_sem=ss, recv_sem=rs, device_id=dev, device_id_type=MESH
        )

    barrier = pltpu.get_barrier_semaphore()
    peers = [ydev(k) for k in range(1, N)] + [zdev(k) for k in range(1, N)]
    peers += [xdev(1), xdev(-1), {"dp": 1 - c}]
    for peer in peers:
        pl.semaphore_signal(barrier, inc=1, device_id=peer, device_id_type=MESH)

    local = [
        pltpu.make_async_copy(dw.at[0], WD, w_l.at[0]),
        pltpu.make_async_copy(gw.at[0, pl.ds(pl.multiple_of(t * 896, 128), 896)], WX.at[0, :, 0:128], w_l.at[1]),
        pltpu.make_async_copy(uw.at[0, pl.ds(pl.multiple_of(t * 896, 128), 896)], WX.at[0, :, 128:256], w_l.at[2]),
    ]
    for d in local:
        d.start()

    block = dither_round(tok[...], dit[...], t * tok.shape[1])
    XA[0, 0] = block[:HALF]
    XB[0, 0] = block[HALF:]
    AUX[0, 0] = gate_table(ids[...], gat[...])
    pl.semaphore_wait(barrier, len(peers))

    sent = []
    counter = [0]

    def go(src, dst, rs, dev):
        d = copy(src, dst, ag_s.at[counter[0]], ag_r.at[rs], dev)
        counter[0] += 1
        d.start()
        sent.append(d)

    def landed(ref, rs):
        pltpu.make_async_copy(ref, ref, ag_r.at[rs]).wait()

    A1, U1, B1 = 0, 8, 16
    A2, B2, U2 = 24, 40, 56

    def first_hop(k):
        h = k // 4
        go(XA.at[0, k], XA.at[1, k], A2 + 2 + h, zdev(1))
        go(XA.at[0, k], XA.at[7, k], A2 + 14 + h, zdev(-1))
        go(XB.at[0, k], XB.at[1, k], B2 + 2 + h, ydev(1))
        go(XB.at[0, k], XB.at[7, k], B2 + 14 + h, ydev(-1))

    def small(src, dst, sign):
        go(XA.at[0, src], XA.at[0, dst], A1 + dst, ydev(sign))
        go(AUX.at[0, src], AUX.at[0, dst], U1 + dst, ydev(sign))
        go(XB.at[0, src], XB.at[0, dst], B1 + dst, zdev(sign))

    def small_landed(k):
        landed(XA.at[0, k], A1 + k)
        landed(AUX.at[0, k], U1 + k)
        landed(XB.at[0, k], B1 + k)

    small(0, 1, 1)
    small(0, 7, -1)
    first_hop(0)

    half = pl.multiple_of(c * 448, 64)
    wide = (slice(0, 128), slice(128, 256))

    def rows_for(k, start, size):
        return pl.ds(pl.multiple_of(((t + k + X) % X) * 896 + c * 448 + start, 32), size)

    near, far = [], []
    for p, w in enumerate((gw, uw)):
        near.append(copy(w.at[0, rows_for(1, 0, 448)], WX.at[3, pl.ds(half, 448), wide[p]], w_s.at[p], w_r.at[p], xdev(1)))
        near.append(copy(w.at[0, rows_for(-1, 0, 448)], WX.at[1, pl.ds(half, 448), wide[p]], w_s.at[2 + p], w_r.at[2 + p], xdev(-1)))
        far.append(copy(w.at[0, rows_for(2, 0, 224)], WF.at[0, :, wide[p]], w_s.at[4 + p], w_r.at[4 + p], xdev(1)))
        far.append(copy(w.at[0, rows_for(2, 224, 224)], WF.at[1, :, wide[p]], w_s.at[6 + p], w_r.at[6 + p], xdev(-1)))
    for d in far + near:
        d.start()
    lower = pl.ds(pl.multiple_of(c * 448, 32), 224)
    upper = pl.ds(pl.multiple_of(c * 448 + 224, 32), 224)
    onward = [
        copy(WF.at[0], WX.at[2, lower], w_s.at[8], w_r.at[8], xdev(1)),
        copy(WF.at[1], WX.at[2, upper], w_s.at[9], w_r.at[9], xdev(-1)),
    ]
    both = [
        copy(WX.at[r, pl.ds(half, 448)], WX.at[r, pl.ds(half, 448)], w_s.at[9 + r], w_r.at[9 + r], {"dp": 1 - c})
        for r in (1, 2, 3)
    ]

    for s in range(1, 5):
        small_landed(s)
        if s < 4:
            small(s, s + 1, 1)
            small_landed(N - s)
            if s < 3:
                small(N - s, N - s - 1, -1)
        first_hop(s)
        if s < 4:
            first_hop(N - s)
    go(AUX.at[0], AUX.at[1], U2 + 1, zdev(1))
    go(AUX.at[0], AUX.at[7], U2 + 7, zdev(-1))

    for d in range(1, 4):
        for h in range(2):
            part = slice(4 * h, 4 * h + 4)
            for big, base, dev in ((XA, A2, zdev), (XB, B2, ydev)):
                landed(big.at[d, part], base + 2 * d + h)
                if d < 3 or h == 0:
                    go(big.at[d, part], big.at[d + 1, part], base + 2 * d + 2 + h, dev(1))
                landed(big.at[N - d, part], base + 2 * (N - d) + h)
                if d < 3 or h == 1:
                    go(big.at[N - d, part], big.at[N - d - 1, part], base + 2 * (N - d - 1) + h, dev(-1))
        landed(AUX.at[d], U2 + d)
        go(AUX.at[d], AUX.at[d + 1], U2 + d + 1, zdev(1))
        landed(AUX.at[N - d], U2 + N - d)
        if d < 3:
            go(AUX.at[N - d], AUX.at[N - d - 1], U2 + N - d - 1, zdev(-1))
        if d == 1:
            for w in far:
                w.wait_recv()
            for w in onward:
                w.start()
            for w in near:
                w.wait_recv()
            both[0].start()
            both[2].start()
        if d == 2:
            for w in onward:
                w.wait_recv()
            both[1].start()
    for h in range(2):
        part = slice(4 * h, 4 * h + 4)
        landed(XA.at[4, part], A2 + 8 + h)
        landed(XB.at[4, part], B2 + 8 + h)
    landed(AUX.at[4], U2 + 4)
    for d in local:
        d.wait()
    for d in both:
        d.wait_recv()

    mine = pl.ds(pl.multiple_of(t * 128, 128), 128)
    left_lanes = pl.ds(pl.multiple_of(((t + 3) % X) * 128, 128), 128)
    right_lanes = pl.ds(pl.multiple_of(((t + 1) % X) * 128, 128), 128)
    lo, hi = pl.ds(0, 64), pl.ds(64, 64)

    def xs(n, k):
        return x_s.at[n * 8 + k], x_r.at[n * 8 + k]

    def d_x1(n):
        return [
            copy(SX.at[n, 1, lo], T1.at[n, lo], *xs(n, 0), xdev(1)),
            copy(SX.at[n, 1, hi], T1.at[n, hi], *xs(n, 1), xdev(-1)),
        ]

    def d_x2(n):
        return [
            copy(SX.at[n, 0], R2.at[n, 0], *xs(n, 2), xdev(1)),
            copy(SX.at[n, 2], R2.at[n, 1], *xs(n, 3), xdev(-1)),
        ]

    def d_h(n):
        return [
            copy(HB.at[n, :, mine], HB.at[n, :, mine], *xs(n, 4), xdev(1)),
            copy(HB.at[n, :, mine], HB.at[n, :, mine], *xs(n, 5), xdev(-1)),
        ]

    def d_hf(n):
        return [
            copy(HB.at[n, lo, left_lanes], HB.at[n, lo, left_lanes], *xs(n, 6), xdev(1)),
            copy(HB.at[n, hi, right_lanes], HB.at[n, hi, right_lanes], *xs(n, 7), xdev(-1)),
        ]

    def d_b(n, h):
        a, b = n * 8 + 2 * h, n * 8 + 2 * h + 1
        if h == 0:
            lefts, rights = (CB.at[n, 4, :, 0:CUT], RB.at[n, 3, :, 0:CUT]), (CB.at[n, 4, :, CUT:896], RB.at[n, 5, :, CUT:896])
        else:
            lefts, rights = (CB.at[n, 4 - h], RB.at[n, 3 - h]), (CB.at[n, 4 + h], RB.at[n, 5 + h])
        return [
            copy(*lefts, b_s.at[a], b_r.at[a], ydev(-1)),
            copy(*rights, b_s.at[b], b_r.at[b], ydev(1)),
        ]

    def d_fb(j):
        return copy(SB.at[j], FB.at[j], fb_s.at[j], fb_r.at[j], zdev(-j))

    def d_fa(k):
        return copy(SA.at[k], FA.at[k], fa_s.at[k], fa_r.at[k], ydev(-k))

    def d_ra0():
        return [
            copy(CA.at[0, lo], RA.at[3, lo], ra_s.at[0], ra_r.at[3], zdev(-1)),
            copy(CA.at[0, hi], RA.at[5, hi], ra_s.at[7], ra_r.at[5], zdev(1)),
        ]

    def d_ra_left(n):
        j = 4 - (n + 1) // 2
        return copy(CA.at[n], RA.at[j - 1], ra_s.at[n], ra_r.at[j - 1], zdev(-1))

    def d_ra_right(n):
        j = 4 + n // 2
        return copy(CA.at[n], RA.at[j + 1], ra_s.at[n], ra_r.at[j + 1], zdev(1))

    def ra_landed(ref, slot):
        pltpu.make_async_copy(ref, ref, ra_r.at[slot]).wait()

    def start(ds):
        for d in ds:
            d.start()

    def arrived(ds):
        for d in ds:
            d.wait_recv()

    def dot(a, b):
        return jnp.dot(a, b, preferred_element_type=F32)

    def s0(n):
        j = group_of(n)
        lane8, sub8 = iota((8, 128), 1), iota((8, 128), 0)
        pick = (sub8 % 4 == e // 8) & (lane8 // HALF == e % 8)
        packed = jnp.zeros((8, 128), F32)
        for k in range(N):
            w = jnp.where(pick, AUX[j, k], 0.0)
            packed = packed + (w if k == 0 else pltpu.roll(w, k * HALF, 1))
        packed = pltpu.roll(packed, ((8 - e % 8) % 8) * HALF, 1)
        g_a = jnp.sum(jnp.where(sub8 < 4, packed, 0.0), axis=0, keepdims=True)
        g_b = jnp.sum(jnp.where(sub8 >= 4, packed, 0.0), axis=0, keepdims=True)
        m_a, m_b = g_a > 0.0, g_b > 0.0
        marks = jnp.concatenate(
            [
                jnp.broadcast_to(jnp.where(m_a, 1.0, 0.0), (8, 128)),
                jnp.broadcast_to(jnp.where(m_b, 1.0, 0.0), (8, 128)),
            ],
            axis=0,
        ).astype(BF)
        r_i, l_i = iota((128, 128), 0), iota((128, 128), 1)
        same = r_i // HALF == l_i // HALF
        before = dot(marks, jnp.where(same & (r_i < l_i), 1.0, 0.0).astype(BF))
        whole = dot(marks, jnp.where(same, 1.0, 0.0).astype(BF))
        base = ((iota((1, 128), 1) // HALF) * HALF).astype(F32)
        code_a = jnp.where(m_a, base + before[0:1], -1.0)
        code_b = jnp.where(m_b, base + before[8:9] + whole[0:1], -1.0)
        row = r_i.astype(F32)
        p_a = jnp.where(code_a == row, 1.0, 0.0)
        p_b = jnp.where(code_b == row, 1.0, 0.0)
        GS[n] = jnp.sum(p_a * g_a + p_b * g_b, axis=1, keepdims=True)
        PT[n, 0:128] = p_a.T.astype(BF)
        PT[n, 128:256] = p_b.T.astype(BF)
        place = jnp.concatenate([p_a, p_b], axis=1).astype(BF)
        rows = jnp.concatenate([XA[j].reshape(128, 896), XB[:, j].reshape(128, 896)], axis=0)
        routed = dot(place, rows).astype(BF)
        SX[n, 1] = dot(routed, WX[2]).astype(BF)
        start(d_x1(n))
        to_right = dot(routed, WX[1])
        NB[n, 0] = to_right[0:64]
        SX[n, 0, 64:128] = to_right[64:128].astype(BF)
        to_left = dot(routed, WX[3])
        NB[n, 1] = to_left[64:128]
        SX[n, 2, 0:64] = to_left[0:64].astype(BF)
        OWN[n] = dot(routed, WX[0])

    def s1(n):
        arrived(d_x1(n))
        SX[n, 0, 0:64] = (NB[n, 0] + T1[n, 0:64].astype(F32)).astype(BF)
        SX[n, 2, 64:128] = (NB[n, 1] + T1[n, 64:128].astype(F32)).astype(BF)
        start(d_x2(n))

    def s2(n):
        arrived(d_x2(n))
        pre = OWN[n] + R2[n, 0].astype(F32) + R2[n, 1].astype(F32)
        gate, up = pre[:, 0:128], pre[:, 128:256]
        HB[n, :, mine] = (gate * jax.nn.sigmoid(gate) * up).astype(BF)
        start(d_h(n))

    def s3(n):
        arrived(d_h(n))
        start(d_hf(n))

    def s4(n):
        arrived(d_hf(n))
        result = (dot(HB[n], WD[...]) * GS[n]).astype(BF)
        back = dot(PT[n], result).astype(BF)
        CA[n] = back[0:128]
        CB[n] = back[128:256].reshape(8, HALF, 896)
        start(d_b(n, 0))

        @pl.when(n == 0)
        def _():
            start(d_ra0())

        @pl.when(n == 1)
        def _():
            ra_landed(RA.at[3, lo], 3)
            CA[1, 0:64] = CA[1, 0:64] + RA[3, 0:64]
            d_ra_left(1).start()

        @pl.when(n == 2)
        def _():
            ra_landed(RA.at[5, hi], 5)
            CA[2, 64:128] = CA[2, 64:128] + RA[5, 64:128]
            d_ra_right(2).start()

        @pl.when((n == 3) | (n == 5))
        def _():
            j = 4 - (n + 1) // 2
            ra_landed(RA.at[j], j)
            CA[n] = CA[n] + RA[j]
            d_ra_left(n).start()

        @pl.when((n == 4) | (n == 6))
        def _():
            j = 4 + n // 2
            ra_landed(RA.at[j], j)
            CA[n] = CA[n] + RA[j]
            d_ra_right(n).start()

        @pl.when(n == 7)
        def _():
            ra_landed(RA.at[0], 0)
            ra_landed(RA.at[8], 8)
            for k in range(7, -1, -1):
                piece = pl.ds(k * HALF, HALF)
                total = CA[7, piece].astype(F32) + RA[0, piece].astype(F32) + RA[8, piece].astype(F32)
                if k == 0:
                    TA[...] = total
                else:
                    SA[k] = total.astype(BF)
                    d_fa(k).start()

    def s5(n, h):
        arrived(d_b(n, h - 1))
        if h == 1:
            CB[n, 3, :, 0:CUT] = CB[n, 3, :, 0:CUT] + RB[n, 3, :, 0:CUT]
            CB[n, 5, :, CUT:896] = CB[n, 5, :, CUT:896] + RB[n, 5, :, CUT:896]
        else:
            CB[n, 4 - h] = CB[n, 4 - h] + RB[n, 4 - h]
            CB[n, 4 + h] = CB[n, 4 + h] + RB[n, 4 + h]
        start(d_b(n, h))

    def s8(n):
        arrived(d_b(n, 3))
        j = group_of(n)
        total = CB[n, 0].astype(F32) + RB[n, 0].astype(F32) + RB[n, 8].astype(F32)

        @pl.when(n < 7)
        def _():
            SB[j] = total.astype(BF)
            d_fb(j).start()

        @pl.when(n == 7)
        def _():
            TB[...] = total

    stages = [
        (3, s3),
        (2, s2),
        (1, s1),
        (0, s0),
        (8, s8),
        (7, functools.partial(s5, h=3)),
        (6, functools.partial(s5, h=2)),
        (5, functools.partial(s5, h=1)),
        (4, s4),
    ]

    def turn(i, carry):
        for lag, stage in stages:

            @pl.when((i >= lag) & (i < lag + GROUPS))
            def _():
                stage(i - lag)

        return carry

    lax.fori_loop(0, GROUPS + 8, turn, 0)

    total_a, total_b = TA[...], TB[...]
    for k in range(1, N):
        d_fa(k).wait_recv()
        total_a = total_a + FA[k].astype(F32)
    for k in range(1, N):
        d_fb(k).wait_recv()
        total_b = total_b + FB[k].astype(F32)
    out[0:HALF] = total_a.astype(BF)
    out[HALF : 2 * HALF] = total_b.astype(BF)

    for d in sent + near + far + onward + both + d_ra0():
        d.wait_send()
    for n in (1, 3, 5):
        d_ra_left(n).wait_send()
    for n in (2, 4, 6):
        d_ra_right(n).wait_send()

    def drain(n, carry):
        for d in d_x1(n) + d_x2(n) + d_h(n) + d_hf(n):
            d.wait_send()
        for h in range(4):
            for d in d_b(n, h):
                d.wait_send()
        return carry

    lax.fori_loop(0, GROUPS, drain, 0)

    def drain_small(k, carry):
        d_fa(k).wait_send()
        d_fb(k).wait_send()
        return carry

    lax.fori_loop(1, N, drain_small, 0)


def on_device(tokens, dither, expert_ids, gate_values, gate_weight, up_weight, down_weight):
    rows, quarter = tokens.shape
    vmem = pl.BlockSpec(memory_space=pltpu.VMEM)
    hbm = pl.BlockSpec(memory_space=pl.ANY)
    dma = pltpu.SemaphoreType.DMA
    return pl.pallas_call(
        kernel,
        out_shape=jax.ShapeDtypeStruct((rows, quarter), BF),
        in_specs=[vmem] * 4 + [hbm] * 3,
        out_specs=vmem,
        scratch_shapes=[
            pltpu.VMEM((8, 8, HALF, 896), BF),
            pltpu.VMEM((8, 8, HALF, 896), BF),
            pltpu.VMEM((8, 8, 8, 128), F32),
            pltpu.VMEM((4, 896, 256), BF),
            pltpu.VMEM((2, 224, 256), BF),
            pltpu.VMEM((512, 896), BF),
            pltpu.VMEM((8, 256, 128), BF),
            pltpu.VMEM((8, 128, 1), F32),
            pltpu.VMEM((8, 128, 256), F32),
            pltpu.VMEM((8, 2, 64, 256), F32),
            pltpu.VMEM((8, 3, 128, 256), BF),
            pltpu.VMEM((8, 128, 256), BF),
            pltpu.VMEM((8, 2, 128, 256), BF),
            pltpu.VMEM((8, 128, 512), BF),
            pltpu.VMEM((8, 128, 896), BF),
            pltpu.VMEM((9, 128, 896), BF),
            pltpu.VMEM((8, 8, HALF, 896), BF),
            pltpu.VMEM((8, 9, HALF, 896), BF),
            pltpu.VMEM((8, HALF, 896), BF),
            pltpu.VMEM((8, HALF, 896), BF),
            pltpu.VMEM((8, HALF, 896), BF),
            pltpu.VMEM((8, HALF, 896), BF),
            pltpu.VMEM((HALF, 896), F32),
            pltpu.VMEM((HALF, 896), F32),
            dma((96,)),
            dma((64,)),
            dma((13,)),
            dma((13,)),
            dma((3,)),
            dma((64,)),
            dma((64,)),
            dma((8,)),
            dma((9,)),
            dma((64,)),
            dma((64,)),
            dma((8,)),
            dma((8,)),
            dma((8,)),
            dma((8,)),
        ],
        compiler_params=pltpu.CompilerParams(
            collective_id=0, has_side_effects=True, vmem_limit_bytes=48 * 1024 * 1024
        ),
        cost_estimate=pl.CostEstimate(flops=5_000_000_000, bytes_accessed=4_000_000, transcendentals=200_000),
    )(tokens, dither.reshape(1, rows), expert_ids, gate_values, gate_weight, up_weight, down_weight)


def solution(mesh):
    in_specs = (
        P(("dp", "expert"), "tensor"),
        P(("dp", "expert")),
        P(("dp", "expert"), None),
        P(("dp", "expert"), None),
        P("expert", None, "tensor"),
        P("expert", None, "tensor"),
        P("expert", None, "tensor"),
    )
    return jax.shard_map(
        on_device, mesh=mesh, in_specs=in_specs, out_specs=P(("dp", "expert"), "tensor"), check_vma=False
    )
```

time: 318 us -> 126 us (0.40)
  the two profiles are of different devices: /device:TPU:4 before, /device:TPU:24 now
where the time goes in v1:
time: 126 us
  Pallas kernels  120 us (95%)
  local copies, waits for them, and re-layouts  6.41 us (5%)
    pallas_call x1, Pallas kernels, on_device(): pl.pallas_call(kernel, out_shape=jax.ShapeDtypeStruct((rows, quarter), BF...  120 us
    unnamed x15, local copies, waits for them, and re-layouts  6.41 us

profile of v1, /device:TPU:24, one launch (start us, length us, event | category | flops | bytes accessed | tf_op | source)
XLA Modules:
  0.0 126.0 jit_solution(4099157437129173963)
XLA Ops:
  0.0 0.0 copy-start.5
  0.0 0.8 copy.8.ids
  0.8 0.0 copy-done.5
  0.8 0.0 copy-start.4
  0.8 0.1 copy.9.gat
  0.9 0.6 copy-done.4
  1.4 0.0 copy-start
  1.4 1.2 copy-done
  2.6 0.0 copy-start.1
  2.6 1.2 copy-done.1
  3.8 0.0 copy-start.2
  3.8 1.2 copy-done.2
  5.0 0.0 copy-start.3
  5.0 0.8 copy-done.3
  5.8 119.6 %shard_map.73 = bf16[32,896]{1,0:T(8,128)(2,1)S(1)} custom-call(bf16[32,896]{1,0:T(8,128)(2,1)S(1)} %copy-done.3, s32[1,32]{1,0:T(1,128)S(1)} %bitcast.1, s32[32,8]{1,0:T(8,128)S(1)} %copy.8.ids, f32[32,8]{1,0:T(8,128)S(1)} %copy.9.gat, bf16[1,3584,128]{2,1,0:T(8,128)(2,1)S(1)} %copy-done, bf16[1,3584,128]{2,1,0:T(8,128)(2,1)S(1)} %copy-done.1, ...), custom_call_target="tpu_custom_call" | custom-call | flops 5000000000 | bytes 4000000 | tf_op jit(solution)/shard_map/pallas_call | solution.py:494
  125.4 0.6 copy.11
Async XLA Ops:
  0.0 0.8 copy-start.5
  0.8 0.7 copy-start.4
  1.4 1.2 copy-start
  2.6 1.2 copy-start.1
  3.8 1.2 copy-start.2
  5.0 0.8 copy-start.3

commit v2 on v1

v2 whole, which is shorter than its diff:
```python
import functools

import jax
import jax.numpy as jnp
from jax import lax
from jax.experimental import pallas as pl
from jax.experimental.pallas import tpu as pltpu
from jax.sharding import PartitionSpec as P

MESH = pl.DeviceIdType.MESH
BF = jnp.bfloat16
F32 = jnp.float32
N = 8
X = 4
HALF = 16
GROUPS = 8
CUT = 512
NEAREST = (1, 7, 2, 6, 3, 5, 4)
STAGGER = False
LAG = 2
HOP = 2


def iota(shape, axis):
    return lax.broadcasted_iota(jnp.int32, shape, axis)


def dither_round(values, dither_row, column_start):
    rows, cols = values.shape
    scaled = values.astype(F32)
    magnitude = jnp.abs(scaled)
    grid = jnp.full_like(scaled, 2.0**-26)
    inverse = jnp.full_like(scaled, 2.0**26)
    for octave in range(-23, 4):
        above = magnitude >= 2.0**octave
        grid = jnp.where(above, 2.0 ** (octave - 2), grid)
        inverse = jnp.where(above, 2.0 ** (2 - octave), inverse)
    square = jnp.broadcast_to(dither_row.astype(F32), (rows, rows))
    diagonal = iota((rows, rows), 0) == iota((rows, rows), 1)
    column = jnp.sum(jnp.where(diagonal, square, 0.0), axis=1, keepdims=True).astype(jnp.int32)
    offset = (column + 97 * (column_start + iota((rows, cols), 1))) & 255
    jitter = (offset.astype(F32) + 0.5) / 256.0
    return (jnp.floor(scaled * inverse + jitter) * grid).astype(BF)


def gate_table(ids, gates):
    rows = []
    expert = iota((8, 128), 1) // HALF
    for h in range(2):
        part = slice(h * HALF, h * HALF + HALF)
        wide_ids = jnp.concatenate([ids[:, part]] * 8, axis=1)
        wide_gates = jnp.concatenate([gates[:, part]] * 8, axis=1)
        for r in range(4):
            chosen = jnp.where(wide_ids == expert + 8 * r, wide_gates, 0.0)
            rows.append(jnp.sum(chosen, axis=0, keepdims=True))
    return jnp.concatenate(rows, axis=0)


def group_of(n):
    return jnp.where(n % 2 == 1, 4 - (n + 1) // 2, 4 + n // 2)


def kernel(
    tok_h, dit, ids, gat, gw, uw, dw, out,
    TOK, PP, XA, XB, AUX, WX, WF, WD, PT, GS, OWN, NB, SX, T1, R2, HB, CA, RA, CB, RB, FA, FB, SA, SB, TA, TB,
    ag_s, ag_r, w_s, w_r, w_l, x_s, x_r, ra_s, ra_r, b_s, b_r, fa_s, fa_r, fb_s, fb_r, turn_sem,
):
    here = lax.axis_index("expert")
    t = lax.axis_index("tensor")
    c = lax.axis_index("dp")
    y, z = here % N, here // N
    e = here // 2

    def ydev(k):
        return {"expert": z * N + (y + k + N) % N}

    def zdev(k):
        return {"expert": ((z + k + N) % N) * N + y}

    def xdev(k):
        return {"tensor": (t + k + X) % X}

    def copy(src, dst, ss, rs, dev):
        return pltpu.make_async_remote_copy(
            src_ref=src, dst_ref=dst, send_sem=ss, recv_sem=rs, device_id=dev, device_id_type=MESH
        )

    barrier = pltpu.get_barrier_semaphore()
    peers = [ydev(k) for k in range(1, N)] + [zdev(k) for k in range(1, N)]
    peers += [xdev(1), xdev(-1), {"dp": 1 - c}]
    for peer in peers:
        pl.semaphore_signal(barrier, inc=1, device_id=peer, device_id_type=MESH)

    local = [
        pltpu.make_async_copy(dw.at[0], WD, w_l.at[0]),
        pltpu.make_async_copy(gw.at[0, pl.ds(pl.multiple_of(t * 896, 128), 896)], WX.at[0, :, 0:128], w_l.at[1]),
        pltpu.make_async_copy(uw.at[0, pl.ds(pl.multiple_of(t * 896, 128), 896)], WX.at[0, :, 128:256], w_l.at[2]),
    ]
    first = pltpu.make_async_copy(tok_h, TOK, w_l.at[3])
    first.start()
    for d in local:
        d.start()
    AUX[0, 0] = gate_table(ids[...], gat[...])
    first.wait()
    block = dither_round(TOK[...], dit[...], t * TOK.shape[1])
    XA[0, 0] = block[:HALF]
    XB[0, 0] = block[HALF:]
    pl.semaphore_wait(barrier, len(peers))

    def dot(a, b):
        return jnp.dot(a, b, preferred_element_type=F32)

    def prepare(j):
        lane8, sub8 = iota((8, 128), 1), iota((8, 128), 0)
        pick = (sub8 % 4 == e // 8) & (lane8 // HALF == e % 8)
        packed = jnp.zeros((8, 128), F32)
        for k in range(N):
            w = jnp.where(pick, AUX[j, k], 0.0)
            packed = packed + (w if k == 0 else pltpu.roll(w, k * HALF, 1))
        packed = pltpu.roll(packed, ((8 - e % 8) % 8) * HALF, 1)
        g_a = jnp.sum(jnp.where(sub8 < 4, packed, 0.0), axis=0, keepdims=True)
        g_b = jnp.sum(jnp.where(sub8 >= 4, packed, 0.0), axis=0, keepdims=True)
        m_a, m_b = g_a > 0.0, g_b > 0.0
        marks = jnp.concatenate(
            [
                jnp.broadcast_to(jnp.where(m_a, 1.0, 0.0), (8, 128)),
                jnp.broadcast_to(jnp.where(m_b, 1.0, 0.0), (8, 128)),
            ],
            axis=0,
        ).astype(BF)
        r_i, l_i = iota((128, 128), 0), iota((128, 128), 1)
        same = r_i // HALF == l_i // HALF
        before = dot(marks, jnp.where(same & (r_i < l_i), 1.0, 0.0).astype(BF))
        whole = dot(marks, jnp.where(same, 1.0, 0.0).astype(BF))
        base = ((iota((1, 128), 1) // HALF) * HALF).astype(F32)
        code_a = jnp.where(m_a, base + before[0:1], -1.0)
        code_b = jnp.where(m_b, base + before[8:9] + whole[0:1], -1.0)
        row = r_i.astype(F32)
        p_a = jnp.where(code_a == row, 1.0, 0.0)
        p_b = jnp.where(code_b == row, 1.0, 0.0)
        GS[j] = jnp.sum(p_a * g_a + p_b * g_b, axis=1, keepdims=True)
        PT[j, 0:128] = p_a.T.astype(BF)
        PT[j, 128:256] = p_b.T.astype(BF)
        PP[j] = jnp.concatenate([p_a, p_b], axis=1).astype(BF)
    sent = []
    counter = [0]

    def go(src, dst, rs, dev):
        d = copy(src, dst, ag_s.at[counter[0]], ag_r.at[rs], dev)
        counter[0] += 1
        d.start()
        sent.append(d)

    def landed(ref, rs):
        pltpu.make_async_copy(ref, ref, ag_r.at[rs]).wait()

    A1, U1, B1 = 0, 8, 16
    A2, B2, U2 = 24, 40, 56

    def first_hop(k):
        h = k // 4
        go(XA.at[0, k], XA.at[1, k], A2 + 2 + h, zdev(1))
        go(XA.at[0, k], XA.at[7, k], A2 + 14 + h, zdev(-1))
        go(XB.at[0, k], XB.at[1, k], B2 + 2 + h, ydev(1))
        go(XB.at[0, k], XB.at[7, k], B2 + 14 + h, ydev(-1))

    def small_landed(k):
        landed(XA.at[0, k], A1 + k)
        landed(AUX.at[0, k], U1 + k)
        landed(XB.at[0, k], B1 + k)

    for k in NEAREST:
        go(XA.at[0, 0], XA.at[0, k], A1 + k, ydev(k))
        go(AUX.at[0, 0], AUX.at[0, k], U1 + k, ydev(k))
        go(XB.at[0, 0], XB.at[0, k], B1 + k, zdev(k))

    half = pl.multiple_of(c * 448, 64)
    wide = (slice(0, 128), slice(128, 256))

    def rows_for(k, start, size):
        return pl.ds(pl.multiple_of(((t + k + X) % X) * 896 + c * 448 + start, 32), size)

    near, far = [], []
    for p, w in enumerate((gw, uw)):
        near.append(copy(w.at[0, rows_for(1, 0, 448)], WX.at[3, pl.ds(half, 448), wide[p]], w_s.at[p], w_r.at[p], xdev(1)))
        near.append(copy(w.at[0, rows_for(-1, 0, 448)], WX.at[1, pl.ds(half, 448), wide[p]], w_s.at[2 + p], w_r.at[2 + p], xdev(-1)))
        far.append(copy(w.at[0, rows_for(2, 0, 224)], WF.at[0, :, wide[p]], w_s.at[4 + p], w_r.at[4 + p], xdev(1)))
        far.append(copy(w.at[0, rows_for(2, 224, 224)], WF.at[1, :, wide[p]], w_s.at[6 + p], w_r.at[6 + p], xdev(-1)))
    for d in far + near:
        d.start()
    lower = pl.ds(pl.multiple_of(c * 448, 32), 224)
    upper = pl.ds(pl.multiple_of(c * 448 + 224, 32), 224)
    onward = [
        copy(WF.at[0], WX.at[2, lower], w_s.at[8], w_r.at[8], xdev(1)),
        copy(WF.at[1], WX.at[2, upper], w_s.at[9], w_r.at[9], xdev(-1)),
    ]
    both = [
        copy(WX.at[r, pl.ds(half, 448)], WX.at[r, pl.ds(half, 448)], w_s.at[9 + r], w_r.at[9 + r], {"dp": 1 - c})
        for r in (1, 2, 3)
    ]

    def recut():
        for w in far:
            w.wait_recv()
        for w in onward:
            w.start()
        for w in near:
            w.wait_recv()
        both[0].start()
        both[2].start()

    def recut_end():
        for w in onward:
            w.wait_recv()
        both[1].start()

    if STAGGER:

        @pl.when(c == 1)
        def _():
            recut()
            recut_end()
            pl.semaphore_wait(turn_sem, 1)

    first_hop(0)
    for k in NEAREST:
        small_landed(k)
        first_hop(k)
    go(AUX.at[0], AUX.at[1], U2 + 1, zdev(1))
    go(AUX.at[0], AUX.at[7], U2 + 7, zdev(-1))

    for d in range(1, 4):
        for h in range(2):
            part = slice(4 * h, 4 * h + 4)
            for big, base, dev in ((XA, A2, zdev), (XB, B2, ydev)):
                landed(big.at[d, part], base + 2 * d + h)
                if d < 3 or h == 0:
                    go(big.at[d, part], big.at[d + 1, part], base + 2 * d + 2 + h, dev(1))
                landed(big.at[N - d, part], base + 2 * (N - d) + h)
                if d < 3 or h == 1:
                    go(big.at[N - d, part], big.at[N - d - 1, part], base + 2 * (N - d - 1) + h, dev(-1))
        landed(AUX.at[d], U2 + d)
        go(AUX.at[d], AUX.at[d + 1], U2 + d + 1, zdev(1))
        landed(AUX.at[N - d], U2 + N - d)
        if d < 3:
            go(AUX.at[N - d], AUX.at[N - d - 1], U2 + N - d - 1, zdev(-1))
        if d == 1:
            if STAGGER:
                pl.when(c == 0)(recut)
            else:
                recut()
            prepare(0)
        if d == 2:
            if STAGGER:
                pl.when(c == 0)(recut_end)
            else:
                recut_end()
        prepare(d)
        prepare(N - d)
    if STAGGER:

        @pl.when(c == 0)
        def _():
            pl.semaphore_signal(turn_sem, inc=1, device_id={"dp": 1 - c}, device_id_type=MESH)

    for h in range(2):
        part = slice(4 * h, 4 * h + 4)
        landed(XA.at[4, part], A2 + 8 + h)
        landed(XB.at[4, part], B2 + 8 + h)
    landed(AUX.at[4], U2 + 4)
    prepare(4)
    for d in local:
        d.wait()
    for d in both:
        d.wait_recv()

    mine = pl.ds(pl.multiple_of(t * 128, 128), 128)
    left_lanes = pl.ds(pl.multiple_of(((t + 3) % X) * 128, 128), 128)
    right_lanes = pl.ds(pl.multiple_of(((t + 1) % X) * 128, 128), 128)
    lo, hi = pl.ds(0, 64), pl.ds(64, 64)

    def xs(n, k):
        return x_s.at[n * 8 + k], x_r.at[n * 8 + k]

    def d_x1(n):
        return [
            copy(SX.at[n, 1, lo], T1.at[n, lo], *xs(n, 0), xdev(1)),
            copy(SX.at[n, 1, hi], T1.at[n, hi], *xs(n, 1), xdev(-1)),
        ]

    def d_x2(n):
        return [
            copy(SX.at[n, 0], R2.at[n, 0], *xs(n, 2), xdev(1)),
            copy(SX.at[n, 2], R2.at[n, 1], *xs(n, 3), xdev(-1)),
        ]

    def d_h(n):
        return [
            copy(HB.at[n, :, mine], HB.at[n, :, mine], *xs(n, 4), xdev(1)),
            copy(HB.at[n, :, mine], HB.at[n, :, mine], *xs(n, 5), xdev(-1)),
        ]

    def d_hf(n):
        return [
            copy(HB.at[n, lo, left_lanes], HB.at[n, lo, left_lanes], *xs(n, 6), xdev(1)),
            copy(HB.at[n, hi, right_lanes], HB.at[n, hi, right_lanes], *xs(n, 7), xdev(-1)),
        ]

    def d_b(n, h):
        a, b = n * 8 + 2 * h, n * 8 + 2 * h + 1
        if h == 0:
            lefts, rights = (CB.at[n, 4, :, 0:CUT], RB.at[n, 3, :, 0:CUT]), (CB.at[n, 4, :, CUT:896], RB.at[n, 5, :, CUT:896])
        else:
            lefts, rights = (CB.at[n, 4 - h], RB.at[n, 3 - h]), (CB.at[n, 4 + h], RB.at[n, 5 + h])
        return [
            copy(*lefts, b_s.at[a], b_r.at[a], ydev(-1)),
            copy(*rights, b_s.at[b], b_r.at[b], ydev(1)),
        ]

    def d_fb(j):
        return copy(SB.at[j], FB.at[j], fb_s.at[j], fb_r.at[j], zdev(-j))

    def d_fa(k):
        return copy(SA.at[k], FA.at[k], fa_s.at[k], fa_r.at[k], ydev(-k))

    def d_ra0():
        return [
            copy(CA.at[0, lo], RA.at[3, lo], ra_s.at[0], ra_r.at[6], zdev(-1)),
            copy(CA.at[0, hi], RA.at[5, hi], ra_s.at[1], ra_r.at[11], zdev(1)),
        ]

    def d_ra_left(n, h):
        j = 4 - (n + 1) // 2
        part = (lo, hi)[h]
        return copy(CA.at[n, part], RA.at[j - 1, part], ra_s.at[2 * n + h], ra_r.at[2 * j - 2 + h], zdev(-1))

    def d_ra_right(n, h):
        j = 4 + n // 2
        part = (lo, hi)[h]
        return copy(CA.at[n, part], RA.at[j + 1, part], ra_s.at[2 * n + h], ra_r.at[2 * j + 2 + h], zdev(1))

    def ra_landed(ref, slot):
        pltpu.make_async_copy(ref, ref, ra_r.at[slot]).wait()

    def start(ds):
        for d in ds:
            d.start()

    def arrived(ds):
        for d in ds:
            d.wait_recv()

    def s0(n):
        j = group_of(n)
        rows = jnp.concatenate([XA[j].reshape(128, 896), XB[:, j].reshape(128, 896)], axis=0)
        routed = dot(PP[j], rows).astype(BF)
        SX[n, 1] = dot(routed, WX[2]).astype(BF)
        start(d_x1(n))
        to_right = dot(routed, WX[1])
        NB[n, 0] = to_right[0:64]
        SX[n, 0, 64:128] = to_right[64:128].astype(BF)
        to_left = dot(routed, WX[3])
        NB[n, 1] = to_left[64:128]
        SX[n, 2, 0:64] = to_left[0:64].astype(BF)
        OWN[n] = dot(routed, WX[0])

    def s1(n):
        arrived(d_x1(n))
        SX[n, 0, 0:64] = (NB[n, 0] + T1[n, 0:64].astype(F32)).astype(BF)
        SX[n, 2, 64:128] = (NB[n, 1] + T1[n, 64:128].astype(F32)).astype(BF)
        start(d_x2(n))

    def s2(n):
        arrived(d_x2(n))
        pre = OWN[n] + R2[n, 0].astype(F32) + R2[n, 1].astype(F32)
        gate, up = pre[:, 0:128], pre[:, 128:256]
        HB[n, :, mine] = (gate * jax.nn.sigmoid(gate) * up).astype(BF)
        start(d_h(n))

    def s3(n):
        arrived(d_h(n))
        start(d_hf(n))

    def s4(n):
        arrived(d_hf(n))
        j = group_of(n)
        result = (dot(HB[n], WD[...]) * GS[j]).astype(BF)
        back = dot(PT[j], result).astype(BF)
        CA[n] = back[0:128]
        CB[n] = back[128:256].reshape(8, HALF, 896)

        start(d_b(n, 0))

        @pl.when(n == 0)
        def _():
            start(d_ra0())

        @pl.when(n % 2 == 1)
        def _():
            j = 4 - (n + 1) // 2

            @pl.when(n < 7)
            def _():
                for h, part in enumerate((lo, hi)):
                    if h == 0:
                        ra_landed(RA.at[j, part], 2 * j + h)
                        CA[n, part] = CA[n, part] + RA[j, part]
                    else:

                        @pl.when(n > 1)
                        def _():
                            ra_landed(RA.at[j, part], 2 * j + h)
                            CA[n, part] = CA[n, part] + RA[j, part]

                    d_ra_left(n, h).start()

        @pl.when((n % 2 == 0) & (n > 0))
        def _():
            j = 4 + n // 2
            for h, part in ((1, hi), (0, lo)):
                if h == 1:
                    ra_landed(RA.at[j, part], 2 * j + h)
                    CA[n, part] = CA[n, part] + RA[j, part]
                else:

                    @pl.when(n > 2)
                    def _():
                        ra_landed(RA.at[j, part], 2 * j + h)
                        CA[n, part] = CA[n, part] + RA[j, part]

                d_ra_right(n, h).start()

        @pl.when(n == 7)
        def _():
            for h, part in enumerate((lo, hi)):
                ra_landed(RA.at[0, part], h)
                ra_landed(RA.at[8, part], 16 + h)
            for k in range(7, -1, -1):
                piece = pl.ds(k * HALF, HALF)
                total = CA[7, piece].astype(F32) + RA[0, piece].astype(F32) + RA[8, piece].astype(F32)
                if k == 0:
                    TA[...] = total
                else:
                    SA[k] = total.astype(BF)
                    d_fa(k).start()

    def s5(n, h):
        arrived(d_b(n, h - 1))
        if h == 1:
            CB[n, 3, :, 0:CUT] = CB[n, 3, :, 0:CUT] + RB[n, 3, :, 0:CUT]
            CB[n, 5, :, CUT:896] = CB[n, 5, :, CUT:896] + RB[n, 5, :, CUT:896]
        else:
            CB[n, 4 - h] = CB[n, 4 - h] + RB[n, 4 - h]
            CB[n, 4 + h] = CB[n, 4 + h] + RB[n, 4 + h]
        start(d_b(n, h))

    def s8(n):
        arrived(d_b(n, 3))
        j = group_of(n)
        total = CB[n, 0].astype(F32) + RB[n, 0].astype(F32) + RB[n, 8].astype(F32)

        @pl.when(n < 7)
        def _():
            SB[j] = total.astype(BF)
            d_fb(j).start()

        @pl.when(n == 7)
        def _():
            TB[...] = total

    last = 4 * LAG
    stages = [
        (1 * LAG, 0, 8, s1),
        (2 * LAG, 0, 8, s2),
        (3 * LAG, 0, 8, s3),
        (0, 0, 8, s0),
        (last, 0, 8, s4),
        (last + 4 * HOP, 0, 8, s8),
        (last + 3 * HOP, 0, 8, functools.partial(s5, h=3)),
        (last + 2 * HOP, 0, 8, functools.partial(s5, h=2)),
        (last + 1 * HOP, 0, 8, functools.partial(s5, h=1)),
    ]
    turns = max(lag + to for lag, _, to, _ in stages)

    def turn(i, carry):
        for lag, since, to, stage in stages:

            @pl.when((i >= lag + since) & (i < lag + to))
            def _():
                stage(i - lag)

        return carry

    lax.fori_loop(0, turns, turn, 0)

    total_a, total_b = TA[...], TB[...]
    for k in range(1, N):
        d_fa(k).wait_recv()
        total_a = total_a + FA[k].astype(F32)
    for k in range(1, N):
        d_fb(k).wait_recv()
        total_b = total_b + FB[k].astype(F32)
    out[0:HALF] = total_a.astype(BF)
    out[HALF : 2 * HALF] = total_b.astype(BF)

    for d in sent + near + far + onward + both + d_ra0():
        d.wait_send()
    for h in range(2):
        for n in (1, 3, 5):
            d_ra_left(n, h).wait_send()
        for n in (2, 4, 6):
            d_ra_right(n, h).wait_send()

    def drain(n, carry):
        for d in d_x1(n) + d_x2(n) + d_h(n) + d_hf(n):
            d.wait_send()

        for h in range(4):
            for d in d_b(n, h):
                d.wait_send()
        return carry

    lax.fori_loop(0, GROUPS, drain, 0)

    def drain_small(k, carry):
        d_fa(k).wait_send()
        d_fb(k).wait_send()
        return carry

    lax.fori_loop(1, N, drain_small, 0)


def on_device(tokens, dither, expert_ids, gate_values, gate_weight, up_weight, down_weight):
    rows, quarter = tokens.shape
    vmem = pl.BlockSpec(memory_space=pltpu.VMEM)
    hbm = pl.BlockSpec(memory_space=pl.ANY)
    dma = pltpu.SemaphoreType.DMA
    return pl.pallas_call(
        kernel,
        out_shape=jax.ShapeDtypeStruct((rows, quarter), BF),
        in_specs=[hbm] + [vmem] * 3 + [hbm] * 3,
        out_specs=vmem,
        scratch_shapes=[
            pltpu.VMEM((rows, quarter), BF),
            pltpu.VMEM((8, 128, 256), BF),
            pltpu.VMEM((8, 8, HALF, 896), BF),
            pltpu.VMEM((8, 8, HALF, 896), BF),
            pltpu.VMEM((8, 8, 8, 128), F32),
            pltpu.VMEM((4, 896, 256), BF),
            pltpu.VMEM((2, 224, 256), BF),
            pltpu.VMEM((512, 896), BF),
            pltpu.VMEM((8, 256, 128), BF),
            pltpu.VMEM((8, 128, 1), F32),
            pltpu.VMEM((8, 128, 256), F32),
            pltpu.VMEM((8, 2, 64, 256), F32),
            pltpu.VMEM((8, 3, 128, 256), BF),
            pltpu.VMEM((8, 128, 256), BF),
            pltpu.VMEM((8, 2, 128, 256), BF),
            pltpu.VMEM((8, 128, 512), BF),
            pltpu.VMEM((8, 128, 896), BF),
            pltpu.VMEM((9, 128, 896), BF),
            pltpu.VMEM((8, 8, HALF, 896), BF),
            pltpu.VMEM((8, 9, HALF, 896), BF),
            pltpu.VMEM((8, HALF, 896), BF),
            pltpu.VMEM((8, HALF, 896), BF),
            pltpu.VMEM((8, HALF, 896), BF),
            pltpu.VMEM((8, HALF, 896), BF),
            pltpu.VMEM((HALF, 896), F32),
            pltpu.VMEM((HALF, 896), F32),
            dma((96,)),
            dma((64,)),
            dma((13,)),
            dma((13,)),
            dma((4,)),
            dma((64,)),
            dma((64,)),
            dma((16,)),
            dma((18,)),
            dma((64,)),
            dma((64,)),
            dma((8,)),
            dma((8,)),
            dma((8,)),
            dma((8,)),
            pltpu.SemaphoreType.REGULAR,
        ],
        compiler_params=pltpu.CompilerParams(
            collective_id=0, has_side_effects=True, vmem_limit_bytes=60 * 1024 * 1024
        ),
        cost_estimate=pl.CostEstimate(flops=5_000_000_000, bytes_accessed=4_000_000, transcendentals=200_000),
    )(tokens, dither.reshape(1, rows), expert_ids.T, gate_values.T, gate_weight, up_weight, down_weight)


def solution(mesh):
    in_specs = (
        P(("dp", "expert"), "tensor"),
        P(("dp", "expert")),
        P(("dp", "expert"), None),
        P(("dp", "expert"), None),
        P("expert", None, "tensor"),
        P("expert", None, "tensor"),
        P("expert", None, "tensor"),
    )
    return jax.shard_map(
        on_device, mesh=mesh, in_specs=in_specs, out_specs=P(("dp", "expert"), "tensor"), check_vma=False
    )
```

time: 126 us -> 114 us (0.905)
  the two profiles are of different devices: /device:TPU:24 before, /device:TPU:2 now
where the time goes in v2:
time: 114 us; the launch traced here: 113 us
  Pallas kernels  112 us (98%)
  local copies, waits for them, and re-layouts  1.45 us (1%)
    pallas_call x1, Pallas kernels, on_device(): pl.pallas_call(kernel, out_shape=jax.ShapeDtypeStruct((rows, quarter), BF...  112 us

profile of v2, /device:TPU:2, one launch (start us, length us, event | category | flops | bytes accessed | tf_op | source)
XLA Modules:
  0.0 113.5 jit_solution(18265648166886014669)
XLA Ops:
  0.0 112.0 %shard_map.73 = bf16[32,896]{1,0:T(8,128)(2,1)} custom-call(bf16[32,896]{1,0:T(8,128)(2,1)} %tok_h.1, s32[1,32]{1,0:T(1,128)} %bitcast.5, s32[8,32]{1,0:T(8,128)} %bitcast.3, f32[8,32]{1,0:T(8,128)} %bitcast.4, bf16[1,3584,128]{2,1,0:T(8,128)(2,1)} %gw.1, bf16[1,3584,128]{2,1,0:T(8,128)(2,1)} %uw.1, bf16[1,512,896]{2,1,0:T(8,128)(2,1)} %dw.1), custom_call_target="tpu_custom_call" | custom-call | flops 5000000000 | bytes 4000000 | tf_op jit(solution)/shard_map/pallas_call | solution.py:538
  112.0 1.4 %copy.9 = bf16[32,896]{1,0:T(8,128)(2,1)} copy(bf16[32,896]{1,0:T(8,128)(2,1)} %shard_map.73) | data formatting | bytes 114688

commit v3 on v2

--- a/solution.py
+++ b/solution.py
@@ -62,7 +62,7 @@
 
 def kernel(
     tok_h, dit, ids, gat, gw, uw, dw, out,
-    TOK, PP, XA, XB, AUX, WX, WF, WD, PT, GS, OWN, NB, SX, T1, R2, HB, CA, RA, CB, RB, FA, FB, SA, SB, TA, TB,
+    TOK, PP, XA, XB, AUX, WX, WF, WD, PT, GS, OWN, SX, R2, HB, CA, RA, CB, RB, FA, FB, SA, SB, TA, TB,
     ag_s, ag_r, w_s, w_r, w_l, x_s, x_r, ra_s, ra_r, b_s, b_r, fa_s, fa_r, fb_s, fb_r, turn_sem,
 ):
     here = lax.axis_index("expert")
@@ -87,7 +87,7 @@
 
     barrier = pltpu.get_barrier_semaphore()
     peers = [ydev(k) for k in range(1, N)] + [zdev(k) for k in range(1, N)]
-    peers += [xdev(1), xdev(-1), {"dp": 1 - c}]
+    peers += [xdev(1), xdev(-1), xdev(2), {"dp": 1 - c}]
     for peer in peers:
         pl.semaphore_signal(barrier, inc=1, device_id=peer, device_id_type=MESH)
 
@@ -275,36 +275,16 @@
         d.wait_recv()
 
     mine = pl.ds(pl.multiple_of(t * 128, 128), 128)
-    left_lanes = pl.ds(pl.multiple_of(((t + 3) % X) * 128, 128), 128)
-    right_lanes = pl.ds(pl.multiple_of(((t + 1) % X) * 128, 128), 128)
     lo, hi = pl.ds(0, 64), pl.ds(64, 64)
 
     def xs(n, k):
         return x_s.at[n * 8 + k], x_r.at[n * 8 + k]
 
-    def d_x1(n):
-        return [
-            copy(SX.at[n, 1, lo], T1.at[n, lo], *xs(n, 0), xdev(1)),
-            copy(SX.at[n, 1, hi], T1.at[n, hi], *xs(n, 1), xdev(-1)),
-        ]
-
-    def d_x2(n):
-        return [
-            copy(SX.at[n, 0], R2.at[n, 0], *xs(n, 2), xdev(1)),
-            copy(SX.at[n, 2], R2.at[n, 1], *xs(n, 3), xdev(-1)),
-        ]
+    def d_x(n):
+        return [copy(SX.at[n, q], R2.at[n, q], *xs(n, q), xdev(k)) for q, k in enumerate((2, 1, -1))]
 
     def d_h(n):
-        return [
-            copy(HB.at[n, :, mine], HB.at[n, :, mine], *xs(n, 4), xdev(1)),
-            copy(HB.at[n, :, mine], HB.at[n, :, mine], *xs(n, 5), xdev(-1)),
-        ]
-
-    def d_hf(n):
-        return [
-            copy(HB.at[n, lo, left_lanes], HB.at[n, lo, left_lanes], *xs(n, 6), xdev(1)),
-            copy(HB.at[n, hi, right_lanes], HB.at[n, hi, right_lanes], *xs(n, 7), xdev(-1)),
-        ]
+        return [copy(HB.at[n, :, mine], HB.at[n, :, mine], *xs(n, 3 + q), xdev(k)) for q, k in enumerate((2, 1, -1))]
 
     def d_b(n, h):
         a, b = n * 8 + 2 * h, n * 8 + 2 * h + 1
@@ -354,35 +334,20 @@
         j = group_of(n)
         rows = jnp.concatenate([XA[j].reshape(128, 896), XB[:, j].reshape(128, 896)], axis=0)
         routed = dot(PP[j], rows).astype(BF)
-        SX[n, 1] = dot(routed, WX[2]).astype(BF)
-        start(d_x1(n))
-        to_right = dot(routed, WX[1])
-        NB[n, 0] = to_right[0:64]
-        SX[n, 0, 64:128] = to_right[64:128].astype(BF)
-        to_left = dot(routed, WX[3])
-        NB[n, 1] = to_left[64:128]
-        SX[n, 2, 0:64] = to_left[0:64].astype(BF)
+        for q, r in enumerate((2, 1, 3)):
+            SX[n, q] = dot(routed, WX[r]).astype(BF)
+            d_x(n)[q].start()
         OWN[n] = dot(routed, WX[0])
 
-    def s1(n):
-        arrived(d_x1(n))
-        SX[n, 0, 0:64] = (NB[n, 0] + T1[n, 0:64].astype(F32)).astype(BF)
-        SX[n, 2, 64:128] = (NB[n, 1] + T1[n, 64:128].astype(F32)).astype(BF)
-        start(d_x2(n))
-
     def s2(n):
-        arrived(d_x2(n))
-        pre = OWN[n] + R2[n, 0].astype(F32) + R2[n, 1].astype(F32)
+        arrived(d_x(n))
+        pre = OWN[n] + R2[n, 0].astype(F32) + R2[n, 1].astype(F32) + R2[n, 2].astype(F32)
         gate, up = pre[:, 0:128], pre[:, 128:256]
         HB[n, :, mine] = (gate * jax.nn.sigmoid(gate) * up).astype(BF)
         start(d_h(n))
 
-    def s3(n):
+    def s4(n):
         arrived(d_h(n))
-        start(d_hf(n))
-
-    def s4(n):
-        arrived(d_hf(n))
         j = group_of(n)
         result = (dot(HB[n], WD[...]) * GS[j]).astype(BF)
         back = dot(PT[j], result).astype(BF)
@@ -468,17 +433,15 @@
         def _():
             TB[...] = total
 
-    last = 4 * LAG
+    last = 2 * LAG
     stages = [
-        (1 * LAG, 0, 8, s1),
-        (2 * LAG, 0, 8, s2),
-        (3 * LAG, 0, 8, s3),
-        (0, 0, 8, s0),
         (last, 0, 8, s4),
         (last + 4 * HOP, 0, 8, s8),
         (last + 3 * HOP, 0, 8, functools.partial(s5, h=3)),
         (last + 2 * HOP, 0, 8, functools.partial(s5, h=2)),
         (last + 1 * HOP, 0, 8, functools.partial(s5, h=1)),
+        (LAG, 0, 8, s2),
+        (0, 0, 8, s0),
     ]
     turns = max(lag + to for lag, _, to, _ in stages)
 
@@ -512,7 +475,7 @@
             d_ra_right(n, h).wait_send()
 
     def drain(n, carry):
-        for d in d_x1(n) + d_x2(n) + d_h(n) + d_hf(n):
+        for d in d_x(n) + d_h(n):
             d.wait_send()
 
         for h in range(4):
@@ -552,10 +515,8 @@
             pltpu.VMEM((8, 256, 128), BF),
             pltpu.VMEM((8, 128, 1), F32),
             pltpu.VMEM((8, 128, 256), F32),
-            pltpu.VMEM((8, 2, 64, 256), F32),
             pltpu.VMEM((8, 3, 128, 256), BF),
-            pltpu.VMEM((8, 128, 256), BF),
-            pltpu.VMEM((8, 2, 128, 256), BF),
+            pltpu.VMEM((8, 3, 128, 256), BF),
             pltpu.VMEM((8, 128, 512), BF),
             pltpu.VMEM((8, 128, 896), BF),
             pltpu.VMEM((9, 128, 896), BF),

time: 114 us -> 112 us (0.982)
  Pallas kernels: 112 us -> 110 us
    pallas_call x1, Pallas kernels: 112 us -> 110 us  [on_device(): pl.pallas_call(kernel, out_shape=jax.ShapeDtypeStruct((rows, quarter), BF...]
where the time goes in v3:
time: 112 us; the launch traced here: 111 us
  Pallas kernels  110 us (98%)
  local copies, waits for them, and re-layouts  1.45 us (1%)
    pallas_call x1, Pallas kernels, on_device(): pl.pallas_call(kernel, out_shape=jax.ShapeDtypeStruct((rows, quarter), BF...  110 us

profile of v3, /device:TPU:2, one launch (start us, length us, event | category | flops | bytes accessed | tf_op | source)
XLA Modules:
  0.0 111.3 jit_solution(1519117585722901836)
XLA Ops:
  0.0 109.9 %shard_map.73 = bf16[32,896]{1,0:T(8,128)(2,1)} custom-call(bf16[32,896]{1,0:T(8,128)(2,1)} %tok_h.1, s32[1,32]{1,0:T(1,128)} %bitcast.5, s32[8,32]{1,0:T(8,128)} %bitcast.3, f32[8,32]{1,0:T(8,128)} %bitcast.4, bf16[1,3584,128]{2,1,0:T(8,128)(2,1)} %gw.1, bf16[1,3584,128]{2,1,0:T(8,128)(2,1)} %uw.1, bf16[1,512,896]{2,1,0:T(8,128)(2,1)} %dw.1), custom_call_target="tpu_custom_call" | custom-call | flops 5000000000 | bytes 4000000 | tf_op jit(solution)/shard_map/pallas_call | solution.py:501
  109.9 1.4 %copy.9 = bf16[32,896]{1,0:T(8,128)(2,1)} copy(bf16[32,896]{1,0:T(8,128)(2,1)} %shard_map.73) | data formatting | bytes 114688

commit v4 on v3

--- a/solution.py
+++ b/solution.py
@@ -400,7 +400,7 @@
             for h, part in enumerate((lo, hi)):
                 ra_landed(RA.at[0, part], h)
                 ra_landed(RA.at[8, part], 16 + h)
-            for k in range(7, -1, -1):
+            for k in (4, 3, 5, 2, 6, 1, 7, 0):
                 piece = pl.ds(k * HALF, HALF)
                 total = CA[7, piece].astype(F32) + RA[0, piece].astype(F32) + RA[8, piece].astype(F32)
                 if k == 0:

time: 112 us -> 111 us (level)
  no operation moved by 1% of the time
where the time goes in v4:
time: 111 us
  Pallas kernels  110 us (99%)
  local copies, waits for them, and re-layouts  1.45 us (1%)
    pallas_call x1, Pallas kernels, on_device(): pl.pallas_call(kernel, out_shape=jax.ShapeDtypeStruct((rows, quarter), BF...  110 us

profile of v4, /device:TPU:2, one launch (start us, length us, event | category | flops | bytes accessed | tf_op | source)
XLA Modules:
  0.0 111.3 jit_solution(10027802067853426228)
XLA Ops:
  0.0 109.8 %shard_map.73 = bf16[32,896]{1,0:T(8,128)(2,1)} custom-call(bf16[32,896]{1,0:T(8,128)(2,1)} %tok_h.1, s32[1,32]{1,0:T(1,128)} %bitcast.5, s32[8,32]{1,0:T(8,128)} %bitcast.3, f32[8,32]{1,0:T(8,128)} %bitcast.4, bf16[1,3584,128]{2,1,0:T(8,128)(2,1)} %gw.1, bf16[1,3584,128]{2,1,0:T(8,128)(2,1)} %uw.1, bf16[1,512,896]{2,1,0:T(8,128)(2,1)} %dw.1), custom_call_target="tpu_custom_call" | custom-call | flops 5000000000 | bytes 4000000 | tf_op jit(solution)/shard_map/pallas_call | solution.py:501
  109.8 1.4 %copy.9 = bf16[32,896]{1,0:T(8,128)(2,1)} copy(bf16[32,896]{1,0:T(8,128)(2,1)} %shard_map.73) | data formatting | bytes 114688
